TPU v7x, 128 devices: a whole 4x4x4 slice. The times are simulated.
128 devices in a mesh: ctx: 4 (over y_lo, core), fsdp: 32 (over z, x, y_hi).
Axes of the slice: x: 4, y: 4 (y_hi: 2, y_lo: 2; y = y_hi * 2 + y_lo), z: 4, core: 2. Of those that a mesh axis runs over, the one named last changes fastest.
Arguments:
- tokens: bfloat16 [32, 2, 4, 128, 896], P('fsdp', None, 'ctx'), may hold values from -6 to 6
- attn_gain: bfloat16 [896], P('fsdp'), may hold values from 0.5 to 1.5
- qkv_weight: bfloat16 [896, 1152], P('fsdp'), may hold values from -0.1875 to 0.1875
- qk_bias: bfloat16 [1024], P('fsdp'), may hold values from -3 to 3
- value_bias: bfloat16 [128], P('fsdp'), may hold values from -3 to 3
- out_weight: bfloat16 [896, 896], P('fsdp'), may hold values from -0.75 to 0.75
- mlp_gain: bfloat16 [896], P('fsdp'), may hold values from 0.5 to 1.5
- gate_weight: bfloat16 [896, 4864], P('fsdp'), may hold values from -0.1875 to 0.1875
- up_weight: bfloat16 [896, 4864], P('fsdp'), may hold values from -0.1875 to 0.1875
- down_weight: bfloat16 [4864, 896], P('fsdp'), may hold values from -0.078125 to 0.078125
- cotangent: bfloat16 [32, 2, 4, 128, 896], P('fsdp', None, 'ctx'), may hold values from -6 to 6
Outputs:
- mixed: bfloat16 [32, 2, 4, 128, 896], P('fsdp', None, 'ctx')
- token_grad: float32 [32, 2, 4, 128, 896], P('fsdp', None, 'ctx')
- attn_gain_grad: float32 [896], P('fsdp')
- qkv_weight_grad: float32 [896, 1152], P('fsdp')
- qk_bias_grad: float32 [1024], P('fsdp')
- value_bias_grad: float32 [128], P('fsdp')
- out_weight_grad: float32 [896, 896], P('fsdp')
- mlp_gain_grad: float32 [896], P('fsdp')
- gate_weight_grad: float32 [896, 4864], P('fsdp')
- up_weight_grad: float32 [896, 4864], P('fsdp')
- down_weight_grad: float32 [4864, 896], P('fsdp')
All inputs are finite; a program needn't handle non-finite values.
Results may differ from a plain program's by a relative error of at most 0.04.
Values may be sent and summed in bfloat16 or wider, within the bound.
No kernel may reach another device: no remote copies, remote signals or barrier semaphores. Data moves between devices by JAX's collectives and lax.ppermute only.
A program may use at most 192 MiB of HBM per device.

v0:
```python
import jax
import jax.numpy as jnp
from jax import lax
from jax.sharding import PartitionSpec as P

H = 14
KVH = 2
HD = 64


EPSILON = 1e-06
THETA = 1000000.0


def shortened(array):
    return jax.tree.map(lambda a: a.astype(jnp.bfloat16) if a.dtype == jnp.float32 else a, array)


def angles(positions, head_dim):
    freqs = THETA ** (-(jnp.arange(head_dim // 2, dtype=jnp.float32) * 2.0 / head_dim))
    return positions.astype(jnp.float32)[:, None] * freqs[None, :]


def rotate(values, turns, direction):
    half = values.shape[-1] // 2
    cosine = jnp.cos(turns)[:, None, :]
    sine = direction * jnp.sin(turns)[:, None, :]
    first = values[..., :half]
    second = values[..., half:]
    return jnp.concatenate(
        [first * cosine - second * sine, second * cosine + first * sine], axis=-1
    )


def rows_inner(left, right):
    return lax.dot_general(
        left, right, (((0,), (0,)), ((), ())), preferred_element_type=jnp.float32
    )


def cols_inner(left, right):
    return lax.dot_general(
        left, right, (((1,), (1,)), ((), ())), preferred_element_type=jnp.float32
    )


def norm_back(grad_normed, normed, inverse):
    return inverse * (grad_normed - normed * jnp.mean(grad_normed * normed, axis=-1, keepdims=True))


def attend_scores(query_heads, key_rows, query_pos, key_pos):
    scale = query_heads.shape[-1] ** (-0.5)
    scores = (
        jnp.einsum("smgrd,skgd->sgrmk", query_heads, key_rows, preferred_element_type=jnp.float32)
        * scale
    )
    causal = query_pos[:, None] >= key_pos[None, :]
    return jnp.where(causal, scores, -1e30)


def shards(
    tokens,
    attn_gain,
    qkv_weight,
    qk_bias,
    value_bias,
    out_weight,
    mlp_gain,
    gate_weight,
    up_weight,
    down_weight,
    cotangent,
):
    ctx_count = lax.axis_size("ctx")
    ctx_here = lax.axis_index("ctx")
    seq_count = tokens.shape[0]
    block_len = tokens.shape[3]
    width = tokens.shape[4]
    row_count = seq_count * 2 * block_len
    ratio = H // KVH
    q_width = H * HD
    k_width = KVH * HD
    key_len = 2 * ctx_count * block_len
    scale = HD ** (-0.5)
    offsets = jnp.arange(block_len, dtype=jnp.int32)
    own_blocks = jnp.stack([ctx_here, 2 * ctx_count - 1 - ctx_here])
    query_pos = (own_blocks[:, None] * block_len + offsets[None, :]).reshape(2 * block_len)
    halves = jnp.arange(2, dtype=jnp.int32)[:, None]
    places = jnp.arange(ctx_count, dtype=jnp.int32)[None, :]
    key_blocks = jnp.where(halves == 0, places, 2 * ctx_count - 1 - places)
    key_pos = (key_blocks[:, :, None] * block_len + offsets[None, None, :]).reshape(key_len)
    row_pos = jnp.broadcast_to(query_pos, (seq_count, 2 * block_len)).reshape(row_count)
    turns = angles(row_pos, HD)
    inputs = tokens.reshape(row_count, width).astype(jnp.float32)
    gain_one, qkv_full, qk_bias_full, value_bias_full, out_full = (
        lax.all_gather(attn_gain, "fsdp", axis=0, tiled=True),
        lax.all_gather(qkv_weight, "fsdp", axis=0, tiled=True),
        lax.all_gather(qk_bias, "fsdp", axis=0, tiled=True),
        lax.all_gather(value_bias, "fsdp", axis=0, tiled=True),
        lax.all_gather(out_weight, "fsdp", axis=0, tiled=True),
    )
    inverse_one = lax.rsqrt(jnp.mean(inputs * inputs, axis=-1, keepdims=True) + EPSILON)
    normed_one = inputs * inverse_one
    normed_in = (normed_one * gain_one.astype(jnp.float32)).astype(jnp.bfloat16)
    bias_full = jnp.concatenate([qk_bias_full, value_bias_full], axis=0).astype(jnp.float32)
    projected = jnp.dot(normed_in, qkv_full, preferred_element_type=jnp.float32) + bias_full
    queries = rotate(projected[:, :q_width].reshape(row_count, H, HD), turns, 1.0).astype(
        jnp.bfloat16
    )
    keys_own = rotate(
        projected[:, q_width : q_width + k_width].reshape(row_count, KVH, HD), turns, 1.0
    ).astype(jnp.bfloat16)
    values_own = projected[:, q_width + k_width :].astype(jnp.bfloat16)
    keys_all, values_all = (
        lax.all_gather(
            keys_own.reshape(seq_count, 2, 1, block_len, k_width), "ctx", axis=2, tiled=True
        ),
        lax.all_gather(
            values_own.reshape(seq_count, 2, 1, block_len, k_width), "ctx", axis=2, tiled=True
        ),
    )
    keys_all = keys_all.reshape(seq_count, key_len, KVH, HD)
    values_all = values_all.reshape(seq_count, key_len, KVH, HD)
    query_heads = queries.reshape(seq_count, 2 * block_len, KVH, ratio, HD)
    scores = attend_scores(query_heads, keys_all, query_pos, key_pos)
    row_max = jnp.max(scores, axis=-1, keepdims=True)
    exp_scores = jnp.exp(scores - row_max)
    row_total = jnp.sum(exp_scores, axis=-1, keepdims=True)
    softmax_out = exp_scores / row_total
    log_total = row_max + jnp.log(row_total)
    attn_rows = jnp.einsum(
        "sgrmk,skgd->smgrd",
        softmax_out.astype(jnp.bfloat16),
        values_all,
        preferred_element_type=jnp.float32,
    )
    attn_rows = attn_rows.reshape(row_count, q_width).astype(jnp.bfloat16)
    hidden = inputs + jnp.dot(attn_rows, out_full, preferred_element_type=jnp.float32)
    gain_two, gate_full, up_full, down_full = (
        lax.all_gather(mlp_gain, "fsdp", axis=0, tiled=True),
        lax.all_gather(gate_weight, "fsdp", axis=0, tiled=True),
        lax.all_gather(up_weight, "fsdp", axis=0, tiled=True),
        lax.all_gather(down_weight, "fsdp", axis=0, tiled=True),
    )
    inverse_two = lax.rsqrt(jnp.mean(hidden * hidden, axis=-1, keepdims=True) + EPSILON)
    normed_two = hidden * inverse_two
    normed_mid = (normed_two * gain_two.astype(jnp.float32)).astype(jnp.bfloat16)
    gate_pre = jnp.dot(normed_mid, gate_full, preferred_element_type=jnp.float32)
    up_pre = jnp.dot(normed_mid, up_full, preferred_element_type=jnp.float32)
    sigmoid_gate = jax.nn.sigmoid(gate_pre)
    silu_gate = gate_pre * sigmoid_gate
    inner = (silu_gate * up_pre).astype(jnp.bfloat16)
    result = hidden + jnp.dot(inner, down_full, preferred_element_type=jnp.float32)
    mixed = result.astype(jnp.bfloat16).reshape(tokens.shape)
    gain_two, gate_full, up_full, down_full = (
        lax.all_gather(mlp_gain, "fsdp", axis=0, tiled=True),
        lax.all_gather(gate_weight, "fsdp", axis=0, tiled=True),
        lax.all_gather(up_weight, "fsdp", axis=0, tiled=True),
        lax.all_gather(down_weight, "fsdp", axis=0, tiled=True),
    )
    out_grad = cotangent.reshape(row_count, width)
    down_grad = rows_inner(inner, out_grad)
    inner_grad = cols_inner(out_grad, down_full)
    gate_grad = (
        inner_grad * up_pre * sigmoid_gate * (1.0 + gate_pre * (1.0 - sigmoid_gate))
    ).astype(jnp.bfloat16)
    up_grad = (inner_grad * silu_gate).astype(jnp.bfloat16)
    gate_wgrad = rows_inner(normed_mid, gate_grad)
    up_wgrad = rows_inner(normed_mid, up_grad)
    mid_grad = cols_inner(gate_grad, gate_full) + cols_inner(up_grad, up_full)
    gain_two_grad = jnp.sum(mid_grad * normed_two, axis=0)
    hidden_grad = out_grad.astype(jnp.float32) + norm_back(
        mid_grad * gain_two.astype(jnp.float32), normed_two, inverse_two
    )
    mlp_terms = (gain_two_grad, gate_wgrad, up_wgrad, down_grad)
    mlp_shares = (
        lax.psum_scatter(
            mlp_terms[0].astype(jnp.bfloat16), "fsdp", scatter_dimension=0, tiled=True
        ).astype(jnp.float32),
        lax.psum_scatter(
            mlp_terms[1].astype(jnp.bfloat16), "fsdp", scatter_dimension=0, tiled=True
        ).astype(jnp.float32),
        lax.psum_scatter(
            mlp_terms[2].astype(jnp.bfloat16), "fsdp", scatter_dimension=0, tiled=True
        ).astype(jnp.float32),
        lax.psum_scatter(
            mlp_terms[3].astype(jnp.bfloat16), "fsdp", scatter_dimension=0, tiled=True
        ).astype(jnp.float32),
    )
    gain_one, qkv_full, qk_bias_full, value_bias_full, out_full = (
        lax.all_gather(attn_gain, "fsdp", axis=0, tiled=True),
        lax.all_gather(qkv_weight, "fsdp", axis=0, tiled=True),
        lax.all_gather(qk_bias, "fsdp", axis=0, tiled=True),
        lax.all_gather(value_bias, "fsdp", axis=0, tiled=True),
        lax.all_gather(out_weight, "fsdp", axis=0, tiled=True),
    )
    branch_grad = hidden_grad.astype(jnp.bfloat16)
    out_wgrad = rows_inner(attn_rows, branch_grad)
    attn_grad = cols_inner(branch_grad, out_full).astype(jnp.bfloat16)
    grad_heads = attn_grad.reshape(seq_count, 2 * block_len, KVH, ratio, HD)
    scores = attend_scores(query_heads, keys_all, query_pos, key_pos)
    softmax_again = jnp.exp(scores - log_total)
    prob_grad = jnp.einsum(
        "smgrd,skgd->sgrmk", grad_heads, values_all, preferred_element_type=jnp.float32
    )
    weighted = jnp.sum(softmax_again * prob_grad, axis=-1, keepdims=True)
    score_grad = (softmax_again * (prob_grad - weighted)).astype(jnp.bfloat16)
    query_grad = (
        jnp.einsum("sgrmk,skgd->smgrd", score_grad, keys_all, preferred_element_type=jnp.float32)
        * scale
    )
    key_grad = (
        jnp.einsum("sgrmk,smgrd->skgd", score_grad, query_heads, preferred_element_type=jnp.float32)
        * scale
    )
    value_grad = jnp.einsum(
        "sgrmk,smgrd->skgd",
        softmax_again.astype(jnp.bfloat16),
        grad_heads,
        preferred_element_type=jnp.float32,
    )
    key_own_grad, value_own_grad = (
        lax.psum_scatter(
            key_grad.reshape(seq_count, 2, ctx_count, block_len, k_width).astype(jnp.bfloat16),
            "ctx",
            scatter_dimension=2,
            tiled=True,
        ).astype(jnp.float32),
        lax.psum_scatter(
            value_grad.reshape(seq_count, 2, ctx_count, block_len, k_width).astype(jnp.bfloat16),
            "ctx",
            scatter_dimension=2,
            tiled=True,
        ).astype(jnp.float32),
    )
    query_back = rotate(query_grad.reshape(row_count, H, HD), turns, -1.0).reshape(
        row_count, q_width
    )
    key_back = rotate(key_own_grad.reshape(row_count, KVH, HD), turns, -1.0).reshape(
        row_count, k_width
    )
    projected_grad = jnp.concatenate(
        [query_back, key_back, value_own_grad.reshape(row_count, k_width)], axis=1
    ).astype(jnp.bfloat16)
    qkv_wgrad = rows_inner(normed_in, projected_grad)
    column_sums = jnp.sum(projected_grad.astype(jnp.float32), axis=0)
    qk_bias_grad = column_sums[: q_width + k_width]
    value_bias_grad = column_sums[q_width + k_width :]
    in_grad = cols_inner(projected_grad, qkv_full)
    gain_one_grad = jnp.sum(in_grad * normed_one, axis=0)
    input_grad = hidden_grad + norm_back(
        in_grad * gain_one.astype(jnp.float32), normed_one, inverse_one
    )
    attn_terms = (gain_one_grad, qkv_wgrad, qk_bias_grad, value_bias_grad, out_wgrad)
    attn_shares = (
        lax.psum_scatter(
            attn_terms[0].astype(jnp.bfloat16), "fsdp", scatter_dimension=0, tiled=True
        ).astype(jnp.float32),
        lax.psum_scatter(
            attn_terms[1].astype(jnp.bfloat16), "fsdp", scatter_dimension=0, tiled=True
        ).astype(jnp.float32),
        lax.psum_scatter(
            attn_terms[2].astype(jnp.bfloat16), "fsdp", scatter_dimension=0, tiled=True
        ).astype(jnp.float32),
        lax.psum_scatter(
            attn_terms[3].astype(jnp.bfloat16), "fsdp", scatter_dimension=0, tiled=True
        ).astype(jnp.float32),
        lax.psum_scatter(
            attn_terms[4].astype(jnp.bfloat16), "fsdp", scatter_dimension=0, tiled=True
        ).astype(jnp.float32),
    )
    summed = jax.tree.map(
        lambda part: part.astype(jnp.float32),
        lax.psum(shortened(tuple(attn_shares) + tuple(mlp_shares)), "ctx"),
    )
    return (
        mixed,
        input_grad.reshape(tokens.shape),
        summed[0],
        summed[1],
        summed[2],
        summed[3],
        summed[4],
        summed[5],
        summed[6],
        summed[7],
        summed[8],
    )


def solution(mesh):
    in_specs = (
        P("fsdp", None, "ctx", None, None),
        P("fsdp"),
        P("fsdp", None),
        P("fsdp"),
        P("fsdp"),
        P("fsdp", None),
        P("fsdp"),
        P("fsdp", None),
        P("fsdp", None),
        P("fsdp", None),
        P("fsdp", None, "ctx", None, None),
    )
    out_specs = (
        P("fsdp", None, "ctx", None, None),
        P("fsdp", None, "ctx", None, None),
        P("fsdp"),
        P("fsdp", None),
        P("fsdp"),
        P("fsdp"),
        P("fsdp", None),
        P("fsdp"),
        P("fsdp", None),
        P("fsdp", None),
        P("fsdp", None),
    )
    return jax.shard_map(shards, mesh=mesh, in_specs=in_specs, out_specs=out_specs, check_vma=False)
```

profile of v0, /device:TPU:1, one launch (start us, length us, event | category | flops | bytes accessed | tf_op | source)
XLA Modules:
  0.0 1545.3 jit_solution(8362445314772506655)
XLA Ops:
  17.3 86.0 %all-reduce.18 = (bf16[896]{0:T(1024)(128)(2,1)S(1)}, bf16[128]{0:T(256)(128)(2,1)S(1)}, bf16[1024]{0:T(1024)(128)(2,1)S(1)}, bf16[896]{0:T(1024)(128)(2,1)S(1)}) all-reduce(bf16[896]{0:T(1024)(128)(2,1)S(1)} %dynamic-update-slice, bf16[128]{0:T(256)(128)(2,1)S(1)} %dynamic-update-slice.2, ...), channel_id=1, replica_groups=mesh['ctx'=4,'fsdp'=32] {'fsdp'}, use_global_device_ids=true, to_apply=%add | all-reduce | flops 2944 | bytes 11776
  109.8 44.6 %all-gather.12.cloned.1.call-done = bf16[32,28,1152]{2,1,0:T(8,128)(2,1)} async-done(((bf16[1,28,1152]{2,1,0:T(8,128)(2,1)}), bf16[32,28,1152]{2,1,0:T(8,128)(2,1)}) %all-gather.12.cloned.1.call-update) | async-done | bytes 2064400 | tf_op jit(solution)/shard_map/all_gather | solution.py:97
  163.7 9.1 all_gather.45
  173.2 6.2 all_gather.44
  182.3 6.7 fusion.47
  189.1 7.1 fusion.7
  196.3 6.8 fusion.18
  204.1 64.7 %all-gather.16.cloned.1.call-done = bf16[32,28,4864]{2,1,0:T(8,128)(2,1)} async-done(((bf16[1,28,4864]{2,1,0:T(8,128)(2,1)}), bf16[32,28,4864]{2,1,0:T(8,128)(2,1)}) %all-gather.16.cloned.1.call-update) | async-done | bytes 8716304 | tf_op jit(solution)/shard_map/all_gather | solution.py:141
  268.8 13.0 reshape.462
  281.8 101.0 %all-gather.18.cloned.1.call-done = bf16[32,28,4864]{2,1,0:T(8,128)(2,1)} async-done(((bf16[1,28,4864]{2,1,0:T(8,128)(2,1)}), bf16[32,28,4864]{2,1,0:T(8,128)(2,1)}) %all-gather.18.cloned.1.call-update) | async-done | bytes 8716304 | tf_op jit(solution)/shard_map/all_gather | solution.py:142
  382.8 12.9 reshape.464
  395.7 8.1 fusion.49
  403.8 4.4 fusion.48
  408.2 81.1 %all-gather.10.cloned.1.call-done = bf16[4864,896]{1,0:T(8,128)(2,1)} async-done(((bf16[152,896]{1,0:T(8,128)(2,1)}), bf16[4864,896]{1,0:T(8,128)(2,1)}) %all-gather.10.cloned.1.call-update) | async-done | bytes 8716304 | tf_op jit(solution)/shard_map/all_gather | solution.py:143
  489.3 11.4 multiply_convert_fusion
  503.6 6.5 multiply_reduce_fusion
  512.6 7.6 fusion.30
  520.2 9.6 fusion.4
  531.0 10.7 fusion.12
  548.5 7.9 convolution_convert_fusion
  557.3 4.7 convolution_multiply_fusion
  564.8 5.9 convolution_convert_fusion.1
  570.7 5.9 convolution_convert_fusion.2
  581.3 694.2 %fusion.45 = (bf16[32,1152]{1,0:T(8,128)(2,1)S(1)}, bf16[32,896]{1,0:T(8,128)(2,1)}, bf16[32,4864]{1,0:T(8,128)(2,1)}, bf16[32,4864]{1,0:T(8,128)(2,1)}) fusion(bf16[896,1152]{1,0:T(8,128)(2,1)S(1)} %convolution_convert_fusion.3, bf16[896,896]{1,0:T(8,128)(2,1)} %convolution_convert_fusion.4, bf16[896,4864]{1,0:T(8,128)(2,1)} %convolution_convert_fusion.2, ...), kind=kCustom, calls=%all-reduce-scatter.4 | all-reduce-scatter fusion | flops 12058625 | bytes 21856768
  1278.5 4.8 collective-permute-start.7
  1295.3 5.5 collective-permute-start.1
  1308.6 76.8 %all-reduce.17 = (bf16[896]{0:T(1024)(128)(2,1)S(1)}, bf16[1024]{0:T(1024)(128)(2,1)S(1)}, bf16[128]{0:T(256)(128)(2,1)S(1)}, bf16[896]{0:T(1024)(128)(2,1)S(1)}) all-reduce(bf16[896]{0:T(1024)(128)(2,1)S(1)} %get-tuple-element.46, bf16[1024]{0:T(1024)(128)(2,1)S(1)} %slice.66, ...), channel_id=4, replica_groups=mesh['ctx'=4,'fsdp'=32] {'fsdp'}, use_global_device_ids=true, to_apply=%region_10.11.clone | all-reduce | flops 2944 | bytes 11776
  1389.3 4.8 collective-permute-start
  1422.0 18.9 %concatenate.48 = bf16[156,4864]{1,0:T(8,128)(2,1)} concatenate(bf16[28,4864]{1,0:T(8,128)(2,1)} %collective-permute-done.11, bf16[32,4864]{1,0:T(8,128)(2,1)} %collective-permute-done.10, bf16[32,4864]{1,0:T(8,128)(2,1)} %collective-permute-done.9, bf16[32,4864]{1,0:T(8,128)(2,1)} %collective-permute-done.8, bf16[32,4864]{1,0:T(8,128)(2,1)S(1)} %copy-done.10), dimensions={0} | concatenate | bytes 3035136
  1442.7 18.5 %concatenate.49 = bf16[156,4864]{1,0:T(8,128)(2,1)} concatenate(bf16[28,4864]{1,0:T(8,128)(2,1)} %collective-permute-done.15, bf16[32,4864]{1,0:T(8,128)(2,1)} %collective-permute-done.14, bf16[32,4864]{1,0:T(8,128)(2,1)S(1)} %collective-permute-done.13, bf16[32,4864]{1,0:T(8,128)(2,1)} %collective-permute-done.12, bf16[32,4864]{1,0:T(8,128)(2,1)S(1)} %copy-done.9), dimensions={0} | concatenate | bytes 3035136
  1463.1 7.9 fusion.17
  1481.5 51.3 %all-reduce.27.cloned.1.call-done = (bf16[28,4864]{1,0:T(8,128)(2,1)}, bf16[28,4864]{1,0:T(8,128)(2,1)}, bf16[152,896]{1,0:T(8,128)(2,1)}) async-done(((bf16[28,4864]{1,0:T(8,128)(2,1)}, bf16[28,4864]{1,0:T(8,128)(2,1)}, bf16[152,896]{1,0:T(8,128)(2,1)}), (bf16[28,4864]{1,0:T(8,128)(2,1)}, bf16[28,4864]{1,0:T(8,128)(2,1)}, bf16[152,896]{1,0:T(8,128)(2,1)})) %all-reduce.27.cloned.1.call-update) | async-done | bytes 817168 | tf_op jit(solution)/shard_map/psum | solution.py:274
  (232 shorter events, 120.7 us)
Async XLA Ops:
  7.2 100.1 %all-gather.14.cloned.1.call-start = ((), (), s32[]{:S(2)}) async-start(), calls=%async_computation.7 | async-start | bytes 1892352 | tf_op jit(solution)/shard_map/all_gather | solution.py:100
  7.9 146.5 %all-gather.12.cloned.1.call-start = ((), (), s32[]{:S(2)}) async-start(), calls=%async_computation.6 | async-start | bytes 2433024 | tf_op jit(solution)/shard_map/all_gather | solution.py:97
  8.7 260.1 %all-gather.16.cloned.1.call-start = ((), (), s32[]{:S(2)}) async-start(), calls=%async_computation.8 | async-start | bytes 10272768 | tf_op jit(solution)/shard_map/all_gather | solution.py:141
  9.4 373.4 %all-gather.18.cloned.1.call-start = ((), (), s32[]{:S(2)}) async-start(), calls=%async_computation.9 | async-start | bytes 10272768 | tf_op jit(solution)/shard_map/all_gather | solution.py:142
  10.0 479.3 %all-gather.10.cloned.1.call-start = ((), (), s32[]{:S(2)}) async-start(), calls=%async_computation.3 | async-start | bytes 8988672 | tf_op jit(solution)/shard_map/all_gather | solution.py:143
  10.6 566.0 %reduce-scatter.17.cloned.1.call-start = ((), (), s32[]{:S(2)}) async-start(), calls=%async_computation.5 | async-start | bytes 327680 | tf_op jit(solution)/shard_map/reduce_scatter | solution.py:229
  105.1 456.9 %copy-start.34 = (f32[256,32]{0,1:T(8,128)}, f32[256,32]{0,1:T(8,128)S(1)}, u32[]{:S(2)}) copy-start(f32[256,32]{0,1:T(8,128)S(1)} %get-tuple-element.84) | copy-start | bytes 98308
  203.9 299.6 %copy-start.4 = (f32[256,896]{1,0:T(8,128)}, f32[256,896]{1,0:T(8,128)S(1)}, u32[]{:S(2)}) copy-start(f32[256,896]{1,0:T(8,128)S(1)} %get-tuple-element.95) | copy-start | bytes 2752516
  403.8 97.0 %slice-start = ((s8[8716288]{0:T(1024)(128)(4,1)}), s8[327680]{0:T(1024)(128)(4,1)S(1)}, s32[]{:S(2)}) async-start(s8[8716288]{0:T(1024)(128)(4,1)} %bitcast.183), calls=%async_computation.13 | async-start | bytes 655360
  530.9 46.7 %reduce-scatter.15.cloned.1.call-start = ((), (), s32[]{:S(2)}) async-start(), calls=%async_computation.4 | async-start | bytes 327680 | tf_op jit(solution)/shard_map/reduce_scatter | solution.py:223
  548.0 915.0 %reduce-scatter.19.cloned.1.call-start = ((), (), s32[]{:S(2)}) async-start(), calls=%async_computation.10 | async-start | bytes 8988672
  556.4 917.5 %all-reduce.25.cloned.1.call-start = ((), (), s32[]{:S(2)}) async-start(), calls=%async_computation.11 | async-start | bytes 266240 | tf_op jit(solution)/shard_map/psum | solution.py:274
  1275.6 111.0 %copy-start.10 = (bf16[32,4864]{1,0:T(8,128)(2,1)S(1)}, bf16[32,4864]{1,0:T(8,128)(2,1)}, u32[]{:S(2)}) copy-start(bf16[32,4864]{1,0:T(8,128)(2,1)} %get-tuple-element.71) | copy-start | bytes 933892
  1275.6 111.8 %copy-start.9 = (bf16[32,4864]{1,0:T(8,128)(2,1)S(1)}, bf16[32,4864]{1,0:T(8,128)(2,1)}, u32[]{:S(2)}) copy-start(bf16[32,4864]{1,0:T(8,128)(2,1)} %get-tuple-element.72) | copy-start | bytes 933892
  1275.6 121.2 %copy-start.33 = (bf16[32,896]{1,0:T(8,128)(2,1)S(1)}, bf16[32,896]{1,0:T(8,128)(2,1)}, u32[]{:S(2)}) copy-start(bf16[32,896]{1,0:T(8,128)(2,1)} %get-tuple-element.70) | copy-start | bytes 172036
  1275.6 25.1 %collective-permute-start.6 = (bf16[32,896]{1,0:T(8,128)(2,1)}, bf16[32,896]{1,0:T(8,128)(2,1)S(1)}, u32[]{:S(2)}, u32[]{:S(2)}) collective-permute-start(bf16[32,896]{1,0:T(8,128)(2,1)} %get-tuple-element.70), channel_id=1, source_target_pairs={{0,3},{1,4},{2,5},{3,6},{4,7},{5,8},{6,9},{7,10},{8,11},{9,12},{10... | collective-permute-start | bytes 172040
  1278.5 16.8 %collective-permute-start.7 = (bf16[28,896]{1,0:T(8,128)(2,1)S(1)}, bf16[28,896]{1,0:T(8,128)(2,1)}, u32[]{:S(2)}, u32[]{:S(2)}) collective-permute-start(bf16[28,896]{1,0:T(8,128)(2,1)S(1)} %slice.69), channel_id=1, source_target_pairs={{0,4},{1,5},{2,6},{3,7},{4,8},{5,9},{6,10},{7,11},{8,12},{9,13},{1... | collective-permute-start | bytes 150536
  1285.9 103.4 %collective-permute-start.5 = (bf16[32,896]{1,0:T(8,128)(2,1)}, bf16[32,896]{1,0:T(8,128)(2,1)S(1)}, u32[]{:S(2)}, u32[]{:S(2)}) collective-permute-start(bf16[32,896]{1,0:T(8,128)(2,1)} %get-tuple-element.70), channel_id=1, source_target_pairs={{0,2},{1,3},{2,4},{3,5},{4,6},{5,7},{6,8},{7,9},{8,10},{9,11},{10,... | collective-permute-start | bytes 172040
  1287.2 107.0 %collective-permute-start.4 = (bf16[32,896]{1,0:T(8,128)(2,1)}, bf16[32,896]{1,0:T(8,128)(2,1)S(1)}, u32[]{:S(2)}, u32[]{:S(2)}) collective-permute-start(bf16[32,896]{1,0:T(8,128)(2,1)} %get-tuple-element.70), channel_id=1, source_target_pairs={{0,1},{1,2},{2,3},{3,4},{4,5},{5,6},{6,7},{7,8},{8,9},{9,10},{10,1... | collective-permute-start | bytes 172040
  1291.4 111.2 %collective-permute-start.2 = (bf16[32,1152]{1,0:T(8,128)(2,1)S(1)}, bf16[32,1152]{1,0:T(8,128)(2,1)S(1)}, u32[]{:S(2)}, u32[]{:S(2)}) collective-permute-start(bf16[32,1152]{1,0:T(8,128)(2,1)S(1)} %get-tuple-element.69), channel_id=1, source_target_pairs={{0,3},{1,4},{2,5},{3,6},{4,7},{5,8},{6,9},{7,10},{8,11},{9,12},{10... | collective-permute-start | bytes 221192
  1295.3 109.3 %collective-permute-start.1 = (bf16[32,1152]{1,0:T(8,128)(2,1)S(1)}, bf16[32,1152]{1,0:T(8,128)(2,1)S(1)}, u32[]{:S(2)}, u32[]{:S(2)}) collective-permute-start(bf16[32,1152]{1,0:T(8,128)(2,1)S(1)} %get-tuple-element.69), channel_id=1, source_target_pairs={{0,2},{1,3},{2,4},{3,5},{4,6},{5,7},{6,8},{7,9},{8,10},{9,11},{10,... | collective-permute-start | bytes 221192
  1300.8 99.8 %collective-permute-start.3 = (bf16[28,1152]{1,0:T(8,128)(2,1)}, bf16[28,1152]{1,0:T(8,128)(2,1)}, u32[]{:S(2)}, u32[]{:S(2)}) collective-permute-start(bf16[28,1152]{1,0:T(8,128)(2,1)} %slice.68), channel_id=1, source_target_pairs={{0,4},{1,5},{2,6},{3,7},{4,8},{5,9},{6,10},{7,11},{8,12},{9,13},{1... | collective-permute-start | bytes 193544
  1389.3 17.9 %collective-permute-start = (bf16[32,1152]{1,0:T(8,128)(2,1)S(1)}, bf16[32,1152]{1,0:T(8,128)(2,1)}, u32[]{:S(2)}, u32[]{:S(2)}) collective-permute-start(bf16[32,1152]{1,0:T(8,128)(2,1)S(1)} %get-tuple-element.69), channel_id=1, source_target_pairs={{0,1},{1,2},{2,3},{3,4},{4,5},{5,6},{6,7},{7,8},{8,9},{9,10},{10,1... | collective-permute-start | bytes 221192
  1394.8 20.9 %collective-permute-start.10 = (bf16[32,4864]{1,0:T(8,128)(2,1)S(1)}, bf16[32,4864]{1,0:T(8,128)(2,1)}, u32[]{:S(2)}, u32[]{:S(2)}) collective-permute-start(bf16[32,4864]{1,0:T(8,128)(2,1)S(1)} %copy-done.10), channel_id=1, source_target_pairs={{0,3},{1,4},{2,5},{3,6},{4,7},{5,8},{6,9},{7,10},{8,11},{9,12},{10... | collective-permute-start | bytes 933896
  1400.5 17.7 %collective-permute-start.9 = (bf16[32,4864]{1,0:T(8,128)(2,1)S(1)}, bf16[32,4864]{1,0:T(8,128)(2,1)}, u32[]{:S(2)}, u32[]{:S(2)}) collective-permute-start(bf16[32,4864]{1,0:T(8,128)(2,1)S(1)} %copy-done.10), channel_id=1, source_target_pairs={{0,2},{1,3},{2,4},{3,5},{4,6},{5,7},{6,8},{7,9},{8,10},{9,11},{10,... | collective-permute-start | bytes 933896
  1402.6 19.4 %collective-permute-start.8 = (bf16[32,4864]{1,0:T(8,128)(2,1)S(1)}, bf16[32,4864]{1,0:T(8,128)(2,1)}, u32[]{:S(2)}, u32[]{:S(2)}) collective-permute-start(bf16[32,4864]{1,0:T(8,128)(2,1)S(1)} %copy-done.10), channel_id=1, source_target_pairs={{0,1},{1,2},{2,3},{3,4},{4,5},{5,6},{6,7},{7,8},{8,9},{9,10},{10,1... | collective-permute-start | bytes 933896
  1404.6 8.0 collective-permute-start.11
  1407.3 35.4 %collective-permute-start.14 = (bf16[32,4864]{1,0:T(8,128)(2,1)S(1)}, bf16[32,4864]{1,0:T(8,128)(2,1)}, u32[]{:S(2)}, u32[]{:S(2)}) collective-permute-start(bf16[32,4864]{1,0:T(8,128)(2,1)S(1)} %copy-done.9), channel_id=1, source_target_pairs={{0,3},{1,4},{2,5},{3,6},{4,7},{5,8},{6,9},{7,10},{8,11},{9,12},{10... | collective-permute-start | bytes 933896
  1412.5 120.3 %all-reduce.27.cloned.1.call-start = ((), (), s32[]{:S(2)}) async-start(), calls=%async_computation.12 | async-start | bytes 1789952 | tf_op jit(solution)/shard_map/psum | solution.py:274
  1412.6 30.1 %collective-permute-start.13 = (bf16[32,4864]{1,0:T(8,128)(2,1)S(1)}, bf16[32,4864]{1,0:T(8,128)(2,1)S(1)}, u32[]{:S(2)}, u32[]{:S(2)}) collective-permute-start(bf16[32,4864]{1,0:T(8,128)(2,1)S(1)} %copy-done.9), channel_id=1, source_target_pairs={{0,2},{1,3},{2,4},{3,5},{4,6},{5,7},{6,8},{7,9},{8,10},{9,11},{10,... | collective-permute-start | bytes 933896
  1415.7 27.0 %collective-permute-start.12 = (bf16[32,4864]{1,0:T(8,128)(2,1)S(1)}, bf16[32,4864]{1,0:T(8,128)(2,1)}, u32[]{:S(2)}, u32[]{:S(2)}) collective-permute-start(bf16[32,4864]{1,0:T(8,128)(2,1)S(1)} %copy-done.9), channel_id=1, source_target_pairs={{0,1},{1,2},{2,3},{3,4},{4,5},{5,6},{6,7},{7,8},{8,9},{9,10},{10,1... | collective-permute-start | bytes 933896
  1418.3 24.4 %collective-permute-start.15 = (bf16[28,4864]{1,0:T(8,128)(2,1)}, bf16[28,4864]{1,0:T(8,128)(2,1)}, u32[]{:S(2)}, u32[]{:S(2)}) collective-permute-start(bf16[28,4864]{1,0:T(8,128)(2,1)} %slice.71), channel_id=1, source_target_pairs={{0,4},{1,5},{2,6},{3,7},{4,8},{5,9},{6,10},{7,11},{8,12},{9,13},{1... | collective-permute-start | bytes 817160
  (36 other events, 769.0 us)
Sparse Core Ops, SparseCore 0:
  11.1 71.7 all-gather.13
  85.9 68.4 all-gather.11
  157.5 111.2 all-gather.15
  271.7 110.9 all-gather.17
  385.6 103.6 all-gather.9
  531.0 15.8 reduce-scatter.16
  549.4 18.2 reduce-scatter.14
  570.1 426.9 reduce-scatter.18
  1412.6 61.2 all-reduce.24
  1477.3 55.4 all-reduce.26
where the time goes:
time: 1550 us
  blocking collectives  872 us (56%)
  waiting for transfers between devices  348 us (22%)
  matrix products  110 us (7%)
  local copies, waits for them, and re-layouts  107 us (7%)
  starting transfers between devices  49.9 us (3%)
  other arithmetic  38.9 us (3%)
  between operations  19.8 us (1%)
    unnamed x3, blocking collectives  857 us
    all_gather x1, waiting for transfers between devices, shards(): lax.all_gather(up_weight, 'fsdp', axis=0, tiled=True)  101 us
    unnamed x113, local copies, waits for them, and re-layouts  96.4 us
    all_gather x1, waiting for transfers between devices, shards(): lax.all_gather(down_weight, 'fsdp', axis=0, tiled=True)  81.1 us
    all_gather x1, waiting for transfers between devices, shards(): lax.all_gather(gate_weight, 'fsdp', axis=0, tiled=True)  64.7 us
    psum x2, waiting for transfers between devices, shards(): lax.psum(shortened(tuple(attn_shares) + tuple(mlp_shares)), 'ctx')  53 us
    unnamed x17, starting transfers between devices  49.6 us
    all_gather x1, waiting for transfers between devices, shards(): lax.all_gather(qkv_weight, 'fsdp', axis=0, tiled=True)  44.6 us
  transfers between devices with their start and end apart: 26, of which 6 were waited for; matrix products, arithmetic and copies ran while one was open for 58% of the time, Pallas kernels for 0%

commit v1 on v0

v1 whole, which is shorter than its diff:
```python
import jax
import jax.numpy as jnp
from jax import lax
from jax.sharding import Mesh, PartitionSpec as P

H = 14
KVH = 2
HD = 64
REP = H // KVH
D = 896
FF = 4864
FFT = FF // 4
QC = REP * HD
PC = QC + 2 * HD
BLK = 128
EPSILON = 1e-06
THETA = 1000000.0
AXES = ("yl", "c", "z", "x", "yh")
BF = jnp.bfloat16
F32 = jnp.float32


def shift(value, axis, size, step):
    return lax.ppermute(value, axis, [(i, (i + step) % size) for i in range(size)])


def swap(value, axis):
    return shift(value, axis, 2, 1)


def angles(positions):
    freqs = THETA ** (-(jnp.arange(HD // 2, dtype=F32) * 2.0 / HD))
    return positions.astype(F32)[:, None] * freqs[None, :]


def rotate(values, cosine, sine):
    half = HD // 2
    first = values[..., :half]
    second = values[..., half:]
    return jnp.concatenate(
        [first * cosine - second * sine, second * cosine + first * sine], axis=-1
    )


def rows_inner(left, right):
    return lax.dot_general(left, right, (((0,), (0,)), ((), ())), preferred_element_type=F32)


def cols_inner(left, right):
    return lax.dot_general(left, right, (((1,), (1,)), ((), ())), preferred_element_type=F32)


def dot(left, right):
    return jnp.dot(left, right, preferred_element_type=F32)


def norm_back(grad_normed, normed, inverse):
    return inverse * (grad_normed - normed * jnp.mean(grad_normed * normed, axis=-1, keepdims=True))


def ordered(own, other, place):
    first = jnp.where(place == 0, own, other)
    second = jnp.where(place == 0, other, own)
    return first, second


def put(pieces, place, size):
    total = jnp.zeros((size,) + pieces[0].shape, pieces[0].dtype)
    for step, piece in enumerate(pieces):
        total = lax.dynamic_update_index_in_dim(total, piece, (place + step) % size, 0)
    return total


def gather4(own, axis, place):
    from_next = shift(own, axis, 4, 3)
    from_last = shift(own, axis, 4, 1)
    from_far = shift(own, axis, 4, 2)
    return put([own, from_next, from_far, from_last], place, 4)


def gather4_ring(own, axis, place):
    half = own.shape[0] // 2
    low, high = own[:half], own[half:]
    low_next, high_next = shift(low, axis, 4, 3), shift(high, axis, 4, 3)
    low_last, high_last = shift(low, axis, 4, 1), shift(high, axis, 4, 1)
    low_far = shift(low_last, axis, 4, 1)
    high_far = shift(high_next, axis, 4, 3)
    lows = put([low, low_next, low_far, low_last], place, 4)
    highs = put([high, high_next, high_far, high_last], place, 4)
    return jnp.concatenate([lows, highs], axis=1)


def scatter4(parts, axis, place):
    def part(step):
        return lax.dynamic_index_in_dim(parts, (place + step) % 4, 0, keepdims=False)

    to_next = shift(part(1), axis, 4, 1)
    to_last = shift(part(3), axis, 4, 3)
    to_far = shift(part(2), axis, 4, 2)
    total = part(0).astype(F32) + to_next.astype(F32) + to_last.astype(F32) + to_far.astype(F32)
    return total.astype(BF)


def scatter2(parts, axis, place):
    keep = lax.dynamic_index_in_dim(parts, place, 0, keepdims=False)
    give = lax.dynamic_index_in_dim(parts, 1 - place, 0, keepdims=False)
    return (keep.astype(F32) + swap(give, axis).astype(F32)).astype(BF)


def plane_from(own, root, place):
    roots = [(r // 2, r % 2, r) for r in range(4)]
    axes = ("yl", "c", "z")

    def flat(yl, c, z):
        return (yl * 2 + c) * 4 + z % 4

    up = lax.ppermute(own, axes, [(flat(a, b, r), flat(a, b, r + 1)) for a, b, r in roots])
    down = lax.ppermute(own, axes, [(flat(a, b, r), flat(a, b, r + 3)) for a, b, r in roots])
    half = own.shape[0] // 2
    far_low = lax.ppermute(
        up[:half], axes, [(flat(a, b, r + 1), flat(a, b, r + 2)) for a, b, r in roots]
    )
    far_high = lax.ppermute(
        down[half:], axes, [(flat(a, b, r + 3), flat(a, b, r + 2)) for a, b, r in roots]
    )
    far = jnp.concatenate([far_low, far_high], axis=0)
    step = (place - root) % 4
    return jnp.where(step == 0, own, jnp.where(step == 1, up, jnp.where(step == 3, down, far)))


def plane_to(own, root, place):
    roots = [(r // 2, r % 2, r) for r in range(4)]
    axes = ("yl", "c", "z")

    def flat(yl, c, z):
        return (yl * 2 + c) * 4 + z % 4

    half = own.shape[0] // 2
    far_low = lax.ppermute(
        own[:half], axes, [(flat(a, b, r + 2), flat(a, b, r + 1)) for a, b, r in roots]
    )
    far_high = lax.ppermute(
        own[half:], axes, [(flat(a, b, r + 2), flat(a, b, r + 3)) for a, b, r in roots]
    )
    joined = own.astype(F32) + jnp.concatenate(
        [far_low.astype(F32), far_high.astype(F32)], axis=0
    )
    joined = joined.astype(BF)
    from_up = lax.ppermute(joined, axes, [(flat(a, b, r + 1), flat(a, b, r)) for a, b, r in roots])
    from_down = lax.ppermute(
        joined, axes, [(flat(a, b, r + 3), flat(a, b, r)) for a, b, r in roots]
    )
    return (own.astype(F32) + from_up.astype(F32) + from_down.astype(F32)).astype(BF)


def shards(
    tokens,
    attn_gain,
    qkv_weight,
    qk_bias,
    value_bias,
    out_weight,
    mlp_gain,
    gate_weight,
    up_weight,
    down_weight,
    cotangent,
):
    yl, c, z, x, yh = [lax.axis_index(name) for name in AXES]
    ctx = yl * 2 + c
    scale = HD ** (-0.5)
    rows = 2 * BLK

    tok = tokens.reshape(rows, D)
    tok_two = jnp.concatenate([tok, swap(tok, "c")], axis=0)
    q_w = D * 1
    qkv_part = jnp.concatenate(
        [
            lax.dynamic_slice_in_dim(qkv_weight, c * QC, QC, 1),
            lax.dynamic_slice_in_dim(qkv_weight, q_w + c * HD, HD, 1),
            lax.dynamic_slice_in_dim(qkv_weight, q_w + KVH * HD + c * HD, HD, 1),
        ],
        axis=1,
    )
    vectors = jnp.concatenate([attn_gain, mlp_gain, qk_bias, value_bias])
    vec_count = vectors.shape[0]
    vec_rows = jnp.zeros((4, PC), BF).at[0, :vec_count].set(vectors)
    packed = jnp.concatenate([qkv_part, vec_rows], axis=0)
    low, high = ordered(packed, swap(packed, "yh"), yh)
    packed = jnp.concatenate([low[:28], high[:28], low[28:], high[28:]], axis=0)
    packed = gather4(packed, "x", x)
    packed = gather4(packed, "z", z)
    qkv_half = packed[:, :, :56].reshape(D, PC)
    vec_all = packed[:, :, 56::4, :vec_count].reshape(32, vec_count).astype(F32)
    gain_one = vec_all[:, :28].reshape(D)
    gain_two = vec_all[:, 28:56].reshape(D)
    qk_bias_full = vec_all[:, 56:88].reshape(D + KVH * HD)
    value_bias_full = vec_all[:, 88:].reshape(KVH * HD)
    bias_part = jnp.concatenate(
        [
            lax.dynamic_slice_in_dim(qk_bias_full, c * QC, QC, 0),
            lax.dynamic_slice_in_dim(qk_bias_full, D + c * HD, HD, 0),
            lax.dynamic_slice_in_dim(value_bias_full, c * HD, HD, 0),
        ]
    )

    def czflat(cc, zz):
        return cc * 4 + zz % 4

    near = lax.ppermute(
        out_weight,
        ("c", "z"),
        [(czflat(a, 2 * a + b), czflat(a, 2 * a + 1 - b)) for a in (0, 1) for b in (0, 1)],
    )
    cross = lax.ppermute(
        out_weight,
        ("c", "z"),
        [(czflat(a, 2 * a), czflat(a, 2 * a + 3)) for a in (0, 1)]
        + [(czflat(a, 2 * a + 1), czflat(a, 2 * a + 2)) for a in (0, 1)],
    )
    cross_near = lax.ppermute(
        cross,
        ("c", "z"),
        [(czflat(a, 2 * a + 3), czflat(a, 2 * a + 2)) for a in (0, 1)]
        + [(czflat(a, 2 * a + 2), czflat(a, 2 * a + 3)) for a in (0, 1)],
    )
    inside = (z // 2) == c
    first_plane = jnp.where(
        inside, jnp.where(z % 2 == 0, out_weight, near), jnp.where(z % 2 == 1, cross, cross_near)
    )
    second_plane = jnp.where(
        inside, jnp.where(z % 2 == 1, out_weight, near), jnp.where(z % 2 == 0, cross, cross_near)
    )
    planes = jnp.stack([first_plane, second_plane])
    low, high = ordered(planes, swap(planes, "yh"), yh)
    planes = jnp.concatenate([low, high], axis=1)
    out_half = jnp.swapaxes(gather4(planes, "x", x), 0, 1).reshape(QC, D)

    gate_part = lax.dynamic_slice_in_dim(gate_weight, ctx * FFT, FFT, 1)
    up_part = lax.dynamic_slice_in_dim(up_weight, ctx * FFT, FFT, 1)
    both = jnp.concatenate([gate_part, up_part], axis=0)
    low, high = ordered(both, swap(both, "yh"), yh)
    gate_part = jnp.concatenate([low[:28], high[:28]], axis=0)
    up_part = jnp.concatenate([low[28:], high[28:]], axis=0)
    gate_t = gather4_ring(gather4(gate_part, "x", x), "z", z).reshape(D, FFT)
    up_rows = gather4(up_part, "z", z)
    up_t = jnp.swapaxes(gather4_ring(up_rows, "x", x), 0, 1).reshape(D, FFT)
    down_part = plane_from(down_weight, ctx, z)
    low, high = ordered(down_part, swap(down_part, "yh"), yh)
    down_part = jnp.concatenate([low, high], axis=0)
    down_t = gather4_ring(down_part, "x", x).reshape(FFT, D)

    offsets = jnp.arange(BLK, dtype=jnp.int32)

    def place_of(place):
        return jnp.concatenate([place * BLK + offsets, (7 - place) * BLK + offsets])

    other_c = yl * 2 + 1 - c
    query_pos = jnp.concatenate([place_of(ctx), place_of(other_c)])
    far_pos = jnp.concatenate([place_of((1 - yl) * 2 + c), place_of((1 - yl) * 2 + 1 - c)])
    key_pos = jnp.concatenate([query_pos, far_pos])
    turns = angles(query_pos)
    cosine, sine = jnp.cos(turns)[:, None, :], jnp.sin(turns)[:, None, :]
    inputs_two = tok_two.astype(F32)
    inverse_one = lax.rsqrt(jnp.mean(inputs_two * inputs_two, axis=-1, keepdims=True) + EPSILON)
    normed_one = inputs_two * inverse_one
    normed_in = (normed_one * gain_one).astype(BF)
    projected = dot(normed_in, qkv_half) + bias_part
    queries = rotate(projected[:, :QC].reshape(2 * rows, REP, HD), cosine, sine).astype(BF)
    key_own = rotate(projected[:, None, QC : QC + HD], cosine, sine)[:, 0].astype(BF)
    value_own = projected[:, QC + HD :].astype(BF)
    kv_own = jnp.concatenate([key_own, value_own], axis=1)
    kv = jnp.concatenate([kv_own, swap(kv_own, "yl")], axis=0)
    keys, values = kv[:, :HD], kv[:, HD:]
    causal = query_pos[:, None] >= key_pos[None, :]
    scores = jnp.einsum("qrd,kd->rqk", queries, keys, preferred_element_type=F32) * scale
    scores = jnp.where(causal, scores, -1e30)
    row_max = jnp.max(scores, axis=-1, keepdims=True)
    exp_scores = jnp.exp(scores - row_max)
    row_total = jnp.sum(exp_scores, axis=-1, keepdims=True)
    prob = exp_scores / row_total
    log_total = row_max + jnp.log(row_total)
    attn = jnp.einsum("rqk,kd->qrd", prob.astype(BF), values, preferred_element_type=F32)
    attn = attn.reshape(2 * rows, QC).astype(BF)
    branch = dot(attn, out_half)
    inputs = inputs_two[:rows]
    hidden = inputs + branch[:rows] + swap(branch[rows:].astype(BF), "c").astype(F32)

    def ctx_gather(own):
        far = swap(own, "yl")
        return jnp.concatenate([own, swap(own, "c"), far, swap(far, "c")], axis=0)

    def ctx_sum(parts):
        parts = parts.reshape(4, rows, D)
        given = swap(jnp.stack([parts[1], parts[3]]).astype(BF), "c").astype(F32)
        far = swap((parts[2] + given[1]).astype(BF), "yl").astype(F32)
        return parts[0] + given[0] + far

    inverse_two = lax.rsqrt(jnp.mean(hidden * hidden, axis=-1, keepdims=True) + EPSILON)
    normed_two = hidden * inverse_two
    normed_mid = ctx_gather((normed_two * gain_two).astype(BF))
    out_grad = cotangent.reshape(rows, D)
    out_grads = ctx_gather(out_grad)
    gate_pre = dot(normed_mid, gate_t)
    up_pre = dot(normed_mid, up_t)
    sigmoid_gate = jax.nn.sigmoid(gate_pre)
    silu_gate = gate_pre * sigmoid_gate
    inner = (silu_gate * up_pre).astype(BF)
    inner_grad = cols_inner(out_grads, down_t)
    gate_grad = (
        inner_grad * up_pre * sigmoid_gate * (1.0 + gate_pre * (1.0 - sigmoid_gate))
    ).astype(BF)
    up_grad = (inner_grad * silu_gate).astype(BF)
    mid_grad = ctx_sum(cols_inner(gate_grad, gate_t) + cols_inner(up_grad, up_t))
    mixed = (hidden + ctx_sum(dot(inner, down_t))).astype(BF)

    down_wgrad = rows_inner(inner, out_grads).astype(BF).reshape(4, 2, 152, D)
    gate_wgrad = rows_inner(normed_mid, gate_grad).astype(BF).reshape(4, 4, 2, 28, FFT)
    up_wgrad = rows_inner(normed_mid, up_grad).astype(BF).reshape(4, 4, 2, 28, FFT)
    down_sum = scatter2(scatter4(down_wgrad, "x", x), "yh", yh)
    down_sum = plane_to(down_sum, ctx, z)
    gate_sum = scatter4(scatter4(gate_wgrad, "z", z), "x", x)
    up_sum = scatter4(scatter4(jnp.swapaxes(up_wgrad, 0, 1), "x", x), "z", z)
    both_sum = scatter2(jnp.concatenate([gate_sum, up_sum], axis=1), "yh", yh)

    def quarters(own):
        near_own = swap(own, "c")
        low, high = ordered(own, near_own, c)
        pair = jnp.stack([low, high])
        low, high = ordered(pair, swap(pair, "yl"), yl)
        return jnp.concatenate([low, high], axis=0)

    both_all = quarters(both_sum).astype(F32)
    both_all = jnp.swapaxes(both_all, 0, 1).reshape(56, FF)
    down_yl = jnp.where(z // 2 == yl, down_sum, swap(down_sum, "yl"))
    down_own = jnp.where(z % 2 == c, down_yl, swap(down_yl, "c")).astype(F32)

    gain_two_grad = jnp.sum(mid_grad * normed_two, axis=0)
    hidden_grad = out_grad.astype(F32) + norm_back(mid_grad * gain_two, normed_two, inverse_two)
    branch_grad = hidden_grad.astype(BF)
    branch_grad = jnp.concatenate([branch_grad, swap(branch_grad, "c")], axis=0)
    out_wgrad = rows_inner(attn, branch_grad).astype(BF).reshape(2, 4, 2, 28, D)
    attn_grad = cols_inner(branch_grad, out_half).astype(BF)
    grad_heads = attn_grad.reshape(2 * rows, REP, HD)
    scores = jnp.einsum("qrd,kd->rqk", queries, keys, preferred_element_type=F32) * scale
    prob = jnp.exp(jnp.where(causal, scores, -1e30) - log_total)
    prob_grad = jnp.einsum("qrd,kd->rqk", grad_heads, values, preferred_element_type=F32)
    weighted = jnp.sum(prob * prob_grad, axis=-1, keepdims=True)
    score_grad = (prob * (prob_grad - weighted)).astype(BF)
    query_grad = jnp.einsum("rqk,kd->qrd", score_grad, keys, preferred_element_type=F32) * scale
    key_grad = jnp.einsum("rqk,qrd->kd", score_grad, queries, preferred_element_type=F32) * scale
    value_grad = jnp.einsum("rqk,qrd->kd", prob.astype(BF), grad_heads, preferred_element_type=F32)
    kv_grad = jnp.concatenate([key_grad, value_grad], axis=1)
    kv_grad = kv_grad[: 2 * rows] + swap(kv_grad[2 * rows :].astype(BF), "yl").astype(F32)
    query_back = rotate(query_grad, cosine, -sine).reshape(2 * rows, QC)
    key_back = rotate(kv_grad[:, None, :HD], cosine, -sine)[:, 0]
    projected_grad = jnp.concatenate([query_back, key_back, kv_grad[:, HD:]], axis=1).astype(BF)
    qkv_wgrad = rows_inner(normed_in, projected_grad).astype(BF)
    bias_grad = jnp.sum(projected_grad.astype(F32), axis=0)
    in_part = cols_inner(projected_grad, qkv_half)
    in_grad = in_part[:rows] + swap(in_part[rows:].astype(BF), "c").astype(F32)
    normed_own = normed_one[:rows]
    gain_one_grad = jnp.sum(in_grad * normed_own, axis=0)
    input_grad = hidden_grad + norm_back(in_grad * gain_one, normed_own, inverse_one[:rows])

    out_sum = scatter2(scatter4(jnp.swapaxes(out_wgrad, 0, 1), "x", x).swapaxes(0, 1), "yh", yh)
    cross_sum = lax.ppermute(
        out_sum,
        ("c", "z"),
        [(czflat(a, 2 * a + 3), czflat(a, 2 * a + 2)) for a in (0, 1)]
        + [(czflat(a, 2 * a + 2), czflat(a, 2 * a + 3)) for a in (0, 1)],
    )
    mine = jnp.where(z % 2 == 1, out_sum[0], out_sum[1]).astype(F32)
    theirs = jnp.where(z % 2 == 1, cross_sum[0], cross_sum[1]).astype(F32)
    collected = (mine + theirs).astype(BF)
    from_out = lax.ppermute(
        collected,
        ("c", "z"),
        [(czflat(a, 2 * a + 3), czflat(a, 2 * a)) for a in (0, 1)]
        + [(czflat(a, 2 * a + 2), czflat(a, 2 * a + 1)) for a in (0, 1)],
    )
    keep = jnp.where(z % 2 == 0, out_sum[0], out_sum[1]).astype(F32)
    give = jnp.where(z % 2 == 0, out_sum[1], out_sum[0])
    from_pair = lax.ppermute(
        give,
        ("c", "z"),
        [(czflat(a, 2 * a + b), czflat(a, 2 * a + 1 - b)) for a in (0, 1) for b in (0, 1)],
    )
    out_own = (keep + from_out.astype(F32) + from_pair.astype(F32)).astype(BF)
    out_own = jnp.where(z // 2 == c, out_own, swap(out_own, "c")).astype(F32)
    out_own = out_own + swap(out_own.astype(BF), "yl").astype(F32)

    zeros_qk = jnp.zeros((D + KVH * HD,), F32)
    qk_grad = lax.dynamic_update_slice(zeros_qk, bias_grad[:QC], (c * QC,))
    qk_grad = lax.dynamic_update_slice(qk_grad, bias_grad[QC : QC + HD], (D + c * HD,))
    value_grad_bias = lax.dynamic_update_slice(
        jnp.zeros((KVH * HD,), F32), bias_grad[QC + HD :], (c * HD,)
    )
    vec_grads = jnp.concatenate(
        [
            gain_one_grad.reshape(32, 28),
            gain_two_grad.reshape(32, 28),
            qk_grad.reshape(32, 32),
            value_grad_bias.reshape(32, 4),
        ],
        axis=1,
    ).astype(BF)
    vec_rows = jnp.zeros((16, 2, 4, PC), BF).at[:, :, 0, :vec_count].set(
        vec_grads.reshape(16, 2, vec_count)
    )
    packed_grad = jnp.concatenate(
        [qkv_wgrad.reshape(16, 56, PC), vec_rows.reshape(16, 8, PC)], axis=1
    ).reshape(4, 4, 64, PC)
    packed_sum = scatter4(scatter4(packed_grad, "z", z), "x", x)
    packed_sum = scatter2(
        jnp.stack(
            [
                jnp.concatenate([packed_sum[:28], packed_sum[56:60]], axis=0),
                jnp.concatenate([packed_sum[28:56], packed_sum[60:]], axis=0),
            ]
        ),
        "yh",
        yh,
    )
    packed_sum = packed_sum.astype(F32) + swap(packed_sum, "yl").astype(F32)
    low, high = ordered(packed_sum, swap(packed_sum.astype(BF), "c").astype(F32), c)
    qkv_own = jnp.concatenate(
        [
            low[:28, :QC],
            high[:28, :QC],
            low[:28, QC : QC + HD],
            high[:28, QC : QC + HD],
            low[:28, QC + HD :],
            high[:28, QC + HD :],
        ],
        axis=1,
    )
    vec_own = low[28, :vec_count] + high[28, :vec_count]

    return (
        mixed.reshape(tokens.shape),
        input_grad.reshape(tokens.shape),
        vec_own[:28],
        qkv_own,
        vec_own[56:88],
        vec_own[88:],
        out_own,
        vec_own[28:56],
        both_all[:28],
        both_all[28:],
        down_own,
    )


def solution(mesh):
    devices = mesh.devices.reshape(2, 2, 4, 4, 2)
    split = Mesh(devices, AXES)
    ctx, fsdp = ("yl", "c"), ("z", "x", "yh")
    rows = P(fsdp, None, ctx, None, None)
    in_specs = (
        rows,
        P(fsdp),
        P(fsdp, None),
        P(fsdp),
        P(fsdp),
        P(fsdp, None),
        P(fsdp),
        P(fsdp, None),
        P(fsdp, None),
        P(fsdp, None),
        rows,
    )
    out_specs = (
        rows,
        rows,
        P(fsdp),
        P(fsdp, None),
        P(fsdp),
        P(fsdp),
        P(fsdp, None),
        P(fsdp),
        P(fsdp, None),
        P(fsdp, None),
        P(fsdp, None),
    )
    return jax.shard_map(
        shards, mesh=split, in_specs=in_specs, out_specs=out_specs, check_vma=False
    )
```

time: 1550 us -> 596 us (0.38)
  blocking collectives: 872 us -> 0 us
  waiting for transfers between devices: 348 us -> 187 us
  starting transfers between devices: 49.9 us -> 204 us
  local copies, waits for them, and re-layouts: 107 us -> 64.9 us
  matrix products: 110 us -> 81.4 us
  between operations: 19.8 us -> 3.37 us
    unnamed x3 -> x0, blocking collectives: 857 us -> none
    all_gather x5 -> x0, waiting for transfers between devices: 291 us -> none  [the longest x1 101 us: shards(): lax.all_gather(up_weight, 'fsdp', axis=0, tiled=True)]
    ppermute x0 -> x103, starting transfers between devices: none -> 204 us  [the longest x89 178 us: shift(): lax.ppermute(value, axis, [(i, (i + step) % size) for i in range(size)])]
    ppermute x0 -> x103, waiting for transfers between devices: none -> 187 us  [the longest x89 180 us: shift(): lax.ppermute(value, axis, [(i, (i + step) % size) for i in range(size)])]
    unnamed x113 -> x153, local copies, waits for them, and re-layouts: 96.4 us -> 7.17 us
    psum x2 -> x0, waiting for transfers between devices: 53 us -> none  [shards(): lax.psum(shortened(tuple(attn_shares) + tuple(mlp_shares)), 'ctx')]
    unnamed x17 -> x0, starting transfers between devices: 49.6 us -> none
    dot_general x11, matrix products: 61.3 us -> 43.2 us  [the longest x5 11.9 us: dot(): return jnp.dot(left, right, preferred_element_type=F32)]
  transfers between devices with their start and end apart: 26 -> 103, of which waited for: 6 -> 47; matrix products, arithmetic and copies ran while one was open for 58% -> 28% of each run, Pallas kernels for 0% -> 0%
where the time goes in v1:
time: 596 us; the launch traced here: 586 us
  starting transfers between devices  204 us (34%)
  waiting for transfers between devices  187 us (31%)
  matrix products  81.4 us (14%)
  local copies, waits for them, and re-layouts  64.9 us (11%)
  other arithmetic  45.6 us (8%)
    ppermute x89, waiting for transfers between devices, shift(): lax.ppermute(value, axis, [(i, (i + step) % size) for i in range(size)])  180 us
    ppermute x89, starting transfers between devices, shift(): lax.ppermute(value, axis, [(i, (i + step) % size) for i in range(size)])  178 us
    dot_general x5, matrix products, cols_inner(): lax.dot_general(left, right, (((1,), (1,)), ((), ())), preferred_element_...  21.6 us
    dot_general x5, matrix products, rows_inner(): lax.dot_general(left, right, (((0,), (0,)), ((), ())), preferred_element_...  16.6 us
    dot_general x5, matrix products, dot(): return jnp.dot(left, right, preferred_element_type=F32)  11.9 us
  transfers between devices with their start and end apart: 103, of which 47 were waited for; matrix products, arithmetic and copies ran while one was open for 28% of the time, Pallas kernels for 0%

profile of v1, /device:TPU:1, one launch (start us, length us, event | category | flops | bytes accessed | tf_op | source)
XLA Modules:
  0.0 585.9 jit_solution(2646067701712957077)
XLA Ops:
  15.7 8.7 %collective-permute-start.11 = (bf16[28,896]{1,0:T(8,128)(2,1)S(1)}, bf16[28,896]{1,0:T(8,128)(2,1)S(1)}, u32[]{:S(2)}, u32[]{:S(2)}) collective-permute-start(bf16[28,896]{1,0:T(8,128)(2,1)S(1)} %collective-permute-done.10), channel_id=1, source_target_pairs={{24,16},{40,32},{16,24},{32,40},{25,17},{41,33},{17,25},{33,41},{2... | collective-permute-start | bytes 150536 | tf_op jit(solution)/shard_map/ppermute | solution.py:221
  87.4 13.7 %collective-permute-start = (bf16[256,896]{1,0:T(8,128)(2,1)S(1)}, bf16[256,896]{1,0:T(8,128)(2,1)S(1)}, u32[]{:S(2)}, u32[]{:S(2)}) collective-permute-start(bf16[256,896]{1,0:T(8,128)(2,1)S(1)} %bitcast.396), channel_id=1, source_target_pairs={{0,32},{32,0},{1,33},{33,1},{2,34},{34,2},{3,35},{35,3},{4,36},{36... | collective-permute-start | bytes 1376264 | tf_op jit(solution)/shard_map/ppermute | solution.py:24
  106.0 7.8 %collective-permute-done.14 = bf16[2,56,896]{2,1,0:T(8,128)(2,1)S(1)} collective-permute-done((bf16[2,56,896]{2,1,0:T(8,128)(2,1)S(1)}, bf16[2,56,896]{2,1,0:T(8,128)(2,1)S(1)}, u32[]{:S(2)}, u32[]{:S(2)}) %collective-permute-start.14) | collective-permute-done | bytes 200736 | tf_op jit(solution)/shard_map/ppermute | solution.py:24
  113.8 6.6 %collective-permute-done.15 = bf16[2,56,896]{2,1,0:T(8,128)(2,1)S(1)} collective-permute-done((bf16[2,56,896]{2,1,0:T(8,128)(2,1)S(1)}, bf16[2,56,896]{2,1,0:T(8,128)(2,1)S(1)}, u32[]{:S(2)}, u32[]{:S(2)}) %collective-permute-start.15) | collective-permute-done | bytes 200736 | tf_op jit(solution)/shard_map/ppermute | solution.py:24
  121.5 7.7 %collective-permute-done.6 = bf16[4,64,576]{2,1,0:T(8,128)(2,1)S(1)} collective-permute-done((bf16[4,64,576]{2,1,0:T(8,128)(2,1)S(1)}, bf16[4,64,576]{2,1,0:T(8,128)(2,1)S(1)}, u32[]{:S(2)}, u32[]{:S(2)}) %collective-permute-start.6) | collective-permute-done | bytes 294944 | tf_op jit(solution)/shard_map/ppermute | solution.py:24
  130.5 8.0 %collective-permute-done.7 = bf16[4,64,576]{2,1,0:T(8,128)(2,1)S(1)} collective-permute-done((bf16[4,64,576]{2,1,0:T(8,128)(2,1)S(1)}, bf16[4,64,576]{2,1,0:T(8,128)(2,1)S(1)}, u32[]{:S(2)}, u32[]{:S(2)}) %collective-permute-start.7) | collective-permute-done | bytes 294944 | tf_op jit(solution)/shard_map/ppermute | solution.py:24
  153.7 6.0 %collective-permute-done.36 = bf16[2,56,1216]{2,1,0:T(8,128)(2,1)S(1)} collective-permute-done((bf16[2,56,1216]{2,1,0:T(8,128)(2,1)}, bf16[2,56,1216]{2,1,0:T(8,128)(2,1)S(1)}, u32[]{:S(2)}, u32[]{:S(2)}) %collective-permute-start.36) | collective-permute-done | bytes 272416 | tf_op jit(solution)/shard_map/ppermute | solution.py:24
  159.8 7.6 %collective-permute-done.24 = bf16[2,56,1216]{2,1,0:T(8,128)(2,1)S(1)} collective-permute-done((bf16[2,56,1216]{2,1,0:T(8,128)(2,1)S(1)}, bf16[2,56,1216]{2,1,0:T(8,128)(2,1)S(1)}, u32[]{:S(2)}, u32[]{:S(2)}) %collective-permute-start.24) | collective-permute-done | bytes 272416 | tf_op jit(solution)/shard_map/ppermute | solution.py:24
  169.0 5.2 collective-permute-done.27
  180.5 6.6 %fusion.129 = (f32[7,512]{1,0:T(8,128)S(1)}, f32[7,512,1024]{1,2,0:T(8,128)}) fusion(bf16[512,7,32]{0,2,1:T(8,128)(2,1)S(1)} %get-tuple-element.133, bf16[512,7,32]{0,2,1:T(8,128)(2,1)S(1)} %get-tuple-element.132, bf16[1024,128]{0,1:T(8,128)(2,1)S(1)} %pad_maximum_fusion.19, pred[512,1024]{0,1:T(8,128)(4,1)S(1)} %copy-done.36), kind=kOutput, calls=%fused_computation.376 | convolution fusion | flops 481686016 | bytes 15808512 | tf_op jit(solution)/shard_map/qrd,kd->rqk/dot_general | solution.py:276
  187.1 7.2 %fusion.3 = f32[7,512]{1,0:T(8,128)S(1)} fusion(f32[7,512,1024]{1,2,0:T(8,128)} %get-tuple-element.199, f32[7,512]{1,0:T(8,128)S(1)} %get-tuple-element.198), kind=kLoop, calls=%fused_computation.9 | loop fusion | flops 7336448 | bytes 14708736 | tf_op jit(solution)/shard_map/reduce_sum | solution.py:280
  194.3 6.7 %fusion.17 = bf16[64,7,512]{2,0,1:T(8,128)(2,1)S(1)} fusion(f32[7,512,1024]{1,2,0:T(8,128)} %get-tuple-element.199, f32[7,512]{1,0:T(8,128)S(1)} %fusion.3, f32[7,512]{1,0:T(8,128)S(1)} %get-tuple-element.198, bf16[1024,128]{0,1:T(8,128)(2,1)S(1)} %pad_maximum_fusion.19), kind=kOutput, calls=%fused_computation.48 | convolution fusion | flops 481001472 | bytes 15302656 | tf_op jit(solution)/shard_map/rqk,kd->qrd/dot_general | solution.py:283
  205.2 5.1 collective-permute-done.25
  210.3 6.8 %collective-permute-start.54 = (bf16[256,896]{1,0:T(8,128)(2,1)}, bf16[256,896]{1,0:T(8,128)(2,1)S(1)}, u32[]{:S(2)}, u32[]{:S(2)}) collective-permute-start(bf16[256,896]{1,0:T(8,128)(2,1)} %collective-permute-done.53), channel_id=1, source_target_pairs={{0,32},{32,0},{1,33},{33,1},{2,34},{34,2},{3,35},{35,3},{4,36},{36... | collective-permute-start | bytes 1376264 | tf_op jit(solution)/shard_map/ppermute | solution.py:24
  217.2 9.6 %collective-permute-done.26 = bf16[2,56,1216]{2,1,0:T(8,128)(2,1)S(1)} collective-permute-done((bf16[2,56,1216]{2,1,0:T(8,128)(2,1)S(1)}, bf16[2,56,1216]{2,1,0:T(8,128)(2,1)S(1)}, u32[]{:S(2)}, u32[]{:S(2)}) %collective-permute-start.26) | collective-permute-done | bytes 272416 | tf_op jit(solution)/shard_map/ppermute | solution.py:24
  229.0 5.4 collective-permute-done.37
  234.4 11.9 %collective-permute-start.28 = (bf16[2,56,1216]{2,1,0:T(8,128)(2,1)S(1)}, bf16[2,56,1216]{2,1,0:T(8,128)(2,1)S(1)}, u32[]{:S(2)}, u32[]{:S(2)}) collective-permute-start(bf16[2,56,1216]{2,1,0:T(8,128)(2,1)S(1)} %collective-permute-done.27), channel_id=1, source_target_pairs={{0,24},{8,0},{16,8},{24,16},{1,25},{9,1},{17,9},{25,17},{2,26},{10... | collective-permute-start | bytes 817160 | tf_op jit(solution)/shard_map/ppermute | solution.py:24
  259.5 5.6 collective-permute-done.44
  269.0 11.6 %collective-permute-done.46 = bf16[152,896]{1,0:T(8,128)(2,1)S(1)} collective-permute-done((bf16[152,896]{1,0:T(8,128)(2,1)S(1)}, bf16[152,896]{1,0:T(8,128)(2,1)S(1)}, u32[]{:S(2)}, u32[]{:S(2)}) %collective-permute-start.46) | collective-permute-done | bytes 272416 | tf_op jit(solution)/shard_map/ppermute | solution.py:24
  280.7 5.9 %collective-permute-start.17 = (bf16[256,896]{1,0:T(8,128)(2,1)S(1)}, bf16[256,896]{1,0:T(8,128)(2,1)S(1)}, u32[]{:S(2)}, u32[]{:S(2)}) collective-permute-start(bf16[256,896]{1,0:T(8,128)(2,1)S(1)} %multiply_convert_fusion.4), channel_id=1, source_target_pairs={{0,32},{32,0},{1,33},{33,1},{2,34},{34,2},{3,35},{35,3},{4,36},{36... | collective-permute-start | bytes 1376264 | tf_op jit(solution)/shard_map/ppermute | solution.py:24
  288.0 7.0 %collective-permute-start.19 = (bf16[256,896]{1,0:T(8,128)(2,1)S(1)}, bf16[256,896]{1,0:T(8,128)(2,1)S(1)}, u32[]{:S(2)}, u32[]{:S(2)}) collective-permute-start(bf16[256,896]{1,0:T(8,128)(2,1)S(1)} %collective-permute-done.18), channel_id=1, source_target_pairs={{0,32},{32,0},{1,33},{33,1},{2,34},{34,2},{3,35},{35,3},{4,36},{36... | collective-permute-start | bytes 1376264 | tf_op jit(solution)/shard_map/ppermute | solution.py:24
  302.0 7.8 %multiply_convert_fusion = (bf16[1024,1216]{0,1:T(8,128)(2,1)S(1)}, bf16[1024,1216]{0,1:T(8,128)(2,1)}, bf16[1024,1216]{0,1:T(8,128)(2,1)S(1)}) fusion(f32[1024,1216]{0,1:T(8,128)S(1)} %fusion.115, f32[1024,1216]{0,1:T(8,128)S(1)} %fusion.114, bf16[1216,896]{1,0:T(8,128)(2,1)S(1)} %bitcast.411, bf16[256,896]{1,0:T(8,128)(2,1)S(1)} %collective-permute-done.54, ...), kind=kOutput, calls=%fused_computation.14 | convolution fusion | flops 2257387520 | bytes 21446656 | tf_op jit(solution)/shard_map/dot_general | solution.py:50
  344.8 4.9 fusion.133
  364.1 5.8 fusion.130
  376.9 10.0 %collective-permute-done.78 = bf16[4,2,28,1216]{3,0,2,1:T(4,128)(2,1)S(1)} collective-permute-done((bf16[4,2,28,1216]{3,0,2,1:T(4,128)(2,1)S(1)}, bf16[4,2,28,1216]{3,0,2,1:T(4,128)(2,1)S(1)}, u32[]{:S(2)}, u32[]{:S(2)}) %collective-permute-start.78) | collective-permute-done | bytes 544800 | tf_op jit(solution)/shard_map/ppermute | solution.py:24
  390.4 8.9 %collective-permute-done.80 = bf16[4,2,28,1216]{3,0,2,1:T(4,128)(2,1)S(1)} collective-permute-done((bf16[4,2,28,1216]{3,0,2,1:T(4,128)(2,1)S(1)}, bf16[4,2,28,1216]{3,0,2,1:T(4,128)(2,1)S(1)}, u32[]{:S(2)}, u32[]{:S(2)}) %collective-permute-start.80) | collective-permute-done | bytes 544800 | tf_op jit(solution)/shard_map/ppermute | solution.py:24
  411.5 5.1 collective-permute-done.82
  416.6 9.1 %collective-permute-start.55 = (bf16[2,256,896]{2,1,0:T(8,128)(2,1)S(1)}, bf16[2,256,896]{2,1,0:T(8,128)(2,1)S(1)}, u32[]{:S(2)}, u32[]{:S(2)}) collective-permute-start(bf16[2,256,896]{2,1,0:T(8,128)(2,1)S(1)} %pad_maximum_fusion.6), channel_id=1, source_target_pairs={{0,32},{32,0},{1,33},{33,1},{2,34},{34,2},{3,35},{35,3},{4,36},{36... | collective-permute-start | bytes 2752520 | tf_op jit(solution)/shard_map/ppermute | solution.py:24
  454.9 9.1 %collective-permute-start.57 = (bf16[256,896]{1,0:T(8,128)(2,1)}, bf16[256,896]{1,0:T(8,128)(2,1)}, u32[]{:S(2)}, u32[]{:S(2)}) collective-permute-start(bf16[256,896]{1,0:T(8,128)(2,1)} %fusion.113), channel_id=1, source_target_pairs={{0,32},{32,0},{1,33},{33,1},{2,34},{34,2},{3,35},{35,3},{4,36},{36... | collective-permute-start | bytes 1376264 | tf_op jit(solution)/shard_map/ppermute | solution.py:24
  473.7 11.9 %fusion = (f32[7,512]{1,0:T(8,128)S(1)}, f32[1024,512,7]{1,0,2:T(8,128)}) fusion(f32[7,512,1024]{1,2,0:T(8,128)} %get-tuple-element.199, f32[7,512]{1,0:T(8,128)S(1)} %copy-done.42, bf16[512,7,64]{0,2,1:T(8,128)(2,1)S(1)} %bitcast.413, bf16[1024,128]{0,1:T(8,128)(2,1)S(1)} %pad_maximum_fusion.19), kind=kOutput, calls=%fused_computation.2 | convolution fusion | flops 480768512 | bytes 29980672 | tf_op jit(solution)/shard_map/qrd,kd->rqk/dot_general | solution.py:347
  490.0 7.1 %fusion.2 = bf16[7,512,1024]{1,2,0:T(8,128)(2,1)S(1)} fusion(f32[1024,512,7]{1,0,2:T(8,128)} %get-tuple-element.203, f32[7,512,1024]{1,2,0:T(8,128)S(1)} %bitcast.393, f32[7,512]{1,0:T(8,128)S(1)} %get-tuple-element.202, f32[7,512]{1,0:T(8,128)S(1)} %copy-done.42), kind=kLoop, calls=%fused_computation.4 | loop fusion | flops 14680064 | bytes 36728832 | tf_op jit(solution)/shard_map/convert_element_type | solution.py:349
  573.7 6.1 %collective-permute-start.68 = (bf16[32,576]{1,0:T(8,128)(2,1)S(1)}, bf16[32,576]{1,0:T(8,128)(2,1)S(1)}, u32[]{:S(2)}, u32[]{:S(2)}) collective-permute-start(bf16[32,576]{1,0:T(8,128)(2,1)S(1)} %fusion.89), channel_id=1, source_target_pairs={{0,32},{32,0},{1,33},{33,1},{2,34},{34,2},{3,35},{35,3},{4,36},{36... | collective-permute-start | bytes 110600 | tf_op jit(solution)/shard_map/ppermute | solution.py:24
  (587 shorter events, 336.3 us)
Async XLA Ops:
  2.1 22.3 %collective-permute-start.9 = (bf16[28,896]{1,0:T(8,128)(2,1)}, bf16[28,896]{1,0:T(8,128)(2,1)S(1)}, u32[]{:S(2)}, u32[]{:S(2)}) collective-permute-start(bf16[28,896]{1,0:T(8,128)(2,1)} %param.20), channel_id=1, source_target_pairs={{0,8},{8,0},{48,56},{56,48},{1,9},{9,1},{49,57},{57,49},{2,10},{10... | collective-permute-start | bytes 150536 | tf_op jit(solution)/shard_map/ppermute | solution.py:210
  2.8 83.8 %collective-permute-start.39 = (bf16[152,896]{1,0:T(8,128)(2,1)}, bf16[152,896]{1,0:T(8,128)(2,1)S(1)}, u32[]{:S(2)}, u32[]{:S(2)}) collective-permute-start(bf16[152,896]{1,0:T(8,128)(2,1)} %param.24), channel_id=1, source_target_pairs={{0,8},{40,48},{80,88},{120,96},{1,9},{41,49},{81,89},{121,97},{2,1... | collective-permute-start | bytes 817160 | tf_op jit(solution)/shard_map/ppermute | solution.py:117
  3.4 99.2 %collective-permute-start.40 = (bf16[152,896]{1,0:T(8,128)(2,1)}, bf16[152,896]{1,0:T(8,128)(2,1)}, u32[]{:S(2)}, u32[]{:S(2)}) collective-permute-start(bf16[152,896]{1,0:T(8,128)(2,1)} %param.24), channel_id=1, source_target_pairs={{0,24},{40,32},{80,72},{120,112},{1,25},{41,33},{81,73},{121,113},... | collective-permute-start | bytes 817160 | tf_op jit(solution)/shard_map/ppermute | solution.py:118
  14.5 189.2 %collective-permute-start.53 = (bf16[256,896]{1,0:T(8,128)(2,1)}, bf16[256,896]{1,0:T(8,128)(2,1)}, u32[]{:S(2)}, u32[]{:S(2)}) collective-permute-start(bf16[256,896]{1,0:T(8,128)(2,1)} %bitcast.89), channel_id=1, source_target_pairs={{0,64},{64,0},{1,65},{65,1},{2,66},{66,2},{3,67},{67,3},{4,68},{68... | collective-permute-start | bytes 1376264 | tf_op jit(solution)/shard_map/ppermute | solution.py:24
  24.4 277.6 %collective-permute-start.52 = (bf16[256,896]{1,0:T(8,128)(2,1)}, bf16[256,896]{1,0:T(8,128)(2,1)}, u32[]{:S(2)}, u32[]{:S(2)}) collective-permute-start(bf16[256,896]{1,0:T(8,128)(2,1)} %bitcast.89), channel_id=1, source_target_pairs={{0,32},{32,0},{1,33},{33,1},{2,34},{34,2},{3,35},{35,3},{4,36},{36... | collective-permute-start | bytes 1376264 | tf_op jit(solution)/shard_map/ppermute | solution.py:24
  83.7 22.3 %collective-permute-start.13 = (bf16[2,56,896]{2,1,0:T(8,128)(2,1)S(1)}, bf16[2,56,896]{2,1,0:T(8,128)(2,1)S(1)}, u32[]{:S(2)}, u32[]{:S(2)}) collective-permute-start(bf16[2,56,896]{2,1,0:T(8,128)(2,1)S(1)} %get-tuple-element.106), channel_id=1, source_target_pairs={{0,6},{2,0},{4,2},{6,4},{1,7},{3,1},{5,3},{7,5},{8,14},{10,8},{12,... | collective-permute-start | bytes 602120 | tf_op jit(solution)/shard_map/ppermute | solution.py:24
  87.4 60.2 %collective-permute-start = (bf16[256,896]{1,0:T(8,128)(2,1)S(1)}, bf16[256,896]{1,0:T(8,128)(2,1)S(1)}, u32[]{:S(2)}, u32[]{:S(2)}) collective-permute-start(bf16[256,896]{1,0:T(8,128)(2,1)S(1)} %bitcast.396), channel_id=1, source_target_pairs={{0,32},{32,0},{1,33},{33,1},{2,34},{34,2},{3,35},{35,3},{4,36},{36... | collective-permute-start | bytes 1376264 | tf_op jit(solution)/shard_map/ppermute | solution.py:24
  102.7 18.5 %collective-permute-start.5 = (bf16[4,64,576]{2,1,0:T(8,128)(2,1)S(1)}, bf16[4,64,576]{2,1,0:T(8,128)(2,1)S(1)}, u32[]{:S(2)}, u32[]{:S(2)}) collective-permute-start(bf16[4,64,576]{2,1,0:T(8,128)(2,1)S(1)} %bitcast_dynamic-update-slice_fusion.40), channel_id=1, source_target_pairs={{0,24},{8,0},{16,8},{24,16},{1,25},{9,1},{17,9},{25,17},{2,26},{10... | collective-permute-start | bytes 884744 | tf_op jit(solution)/shard_map/ppermute | solution.py:24
  121.1 17.4 %collective-permute-start.7 = (bf16[4,64,576]{2,1,0:T(8,128)(2,1)S(1)}, bf16[4,64,576]{2,1,0:T(8,128)(2,1)S(1)}, u32[]{:S(2)}, u32[]{:S(2)}) collective-permute-start(bf16[4,64,576]{2,1,0:T(8,128)(2,1)S(1)} %bitcast_dynamic-update-slice_fusion.40), channel_id=1, source_target_pairs={{0,8},{8,16},{16,24},{24,0},{1,9},{9,17},{17,25},{25,1},{2,10},{10... | collective-permute-start | bytes 884744 | tf_op jit(solution)/shard_map/ppermute | solution.py:24
  144.9 58.3 %collective-permute-start.34 = (bf16[2,56,1216]{2,1,0:T(8,128)(2,1)}, bf16[2,56,1216]{2,1,0:T(8,128)(2,1)S(1)}, u32[]{:S(2)}, u32[]{:S(2)}) collective-permute-start(bf16[2,56,1216]{2,1,0:T(8,128)(2,1)} %get-tuple-element.150), channel_id=1, source_target_pairs={{0,2},{2,4},{4,6},{6,0},{1,3},{3,5},{5,7},{7,1},{8,10},{10,12},{12... | collective-permute-start | bytes 817160 | tf_op jit(solution)/shard_map/ppermute | solution.py:24
  153.6 92.6 %collective-permute-start.38 = (bf16[2,56,1216]{2,1,0:T(8,128)(2,1)S(1)}, bf16[2,56,1216]{2,1,0:T(8,128)(2,1)S(1)}, u32[]{:S(2)}, u32[]{:S(2)}) collective-permute-start(bf16[2,56,1216]{2,1,0:T(8,128)(2,1)S(1)} %copy-done.43), channel_id=1, source_target_pairs={{0,2},{2,4},{4,6},{6,0},{1,3},{3,5},{5,7},{7,1},{8,10},{10,12},{12... | collective-permute-start | bytes 817160 | tf_op jit(solution)/shard_map/ppermute | solution.py:24
  178.0 25.2 %collective-permute-start.43 = (bf16[152,896]{1,0:T(8,128)(2,1)S(1)}, bf16[152,896]{1,0:T(8,128)(2,1)S(1)}, u32[]{:S(2)}, u32[]{:S(2)}) collective-permute-start(bf16[152,896]{1,0:T(8,128)(2,1)S(1)} %fusion.63), channel_id=1, source_target_pairs={{0,1},{1,0},{2,3},{3,2},{4,5},{5,4},{6,7},{7,6},{8,9},{9,8},{10,11... | collective-permute-start | bytes 817160 | tf_op jit(solution)/shard_map/ppermute | solution.py:24
  203.7 52.6 %collective-permute-start.29 = (bf16[2,56,1216]{2,1,0:T(8,128)(2,1)S(1)}, bf16[2,56,1216]{2,1,0:T(8,128)(2,1)S(1)}, u32[]{:S(2)}, u32[]{:S(2)}) collective-permute-start(bf16[2,56,1216]{2,1,0:T(8,128)(2,1)S(1)} %copy-done.44), channel_id=1, source_target_pairs={{0,8},{8,16},{16,24},{24,0},{1,9},{9,17},{17,25},{25,1},{2,10},{10... | collective-permute-start | bytes 817160 | tf_op jit(solution)/shard_map/ppermute | solution.py:24
  210.3 91.7 %collective-permute-start.54 = (bf16[256,896]{1,0:T(8,128)(2,1)}, bf16[256,896]{1,0:T(8,128)(2,1)S(1)}, u32[]{:S(2)}, u32[]{:S(2)}) collective-permute-start(bf16[256,896]{1,0:T(8,128)(2,1)} %collective-permute-done.53), channel_id=1, source_target_pairs={{0,32},{32,0},{1,33},{33,1},{2,34},{34,2},{3,35},{35,3},{4,36},{36... | collective-permute-start | bytes 1376264 | tf_op jit(solution)/shard_map/ppermute | solution.py:24
  234.4 18.3 %collective-permute-start.28 = (bf16[2,56,1216]{2,1,0:T(8,128)(2,1)S(1)}, bf16[2,56,1216]{2,1,0:T(8,128)(2,1)S(1)}, u32[]{:S(2)}, u32[]{:S(2)}) collective-permute-start(bf16[2,56,1216]{2,1,0:T(8,128)(2,1)S(1)} %collective-permute-done.27), channel_id=1, source_target_pairs={{0,24},{8,0},{16,8},{24,16},{1,25},{9,1},{17,9},{25,17},{2,26},{10... | collective-permute-start | bytes 817160 | tf_op jit(solution)/shard_map/ppermute | solution.py:24
  246.3 22.3 %collective-permute-start.16 = (bf16[256,896]{1,0:T(8,128)(2,1)S(1)}, bf16[256,896]{1,0:T(8,128)(2,1)S(1)}, u32[]{:S(2)}, u32[]{:S(2)}) collective-permute-start(bf16[256,896]{1,0:T(8,128)(2,1)S(1)} %slice.614), channel_id=1, source_target_pairs={{0,32},{32,0},{1,33},{33,1},{2,34},{34,2},{3,35},{35,3},{4,36},{36... | collective-permute-start | bytes 1376264 | tf_op jit(solution)/shard_map/ppermute | solution.py:24
  265.1 29.9 %collective-permute-start.49 = (bf16[152,896]{1,0:T(8,128)(2,1)S(1)}, bf16[152,896]{1,0:T(8,128)(2,1)S(1)}, u32[]{:S(2)}, u32[]{:S(2)}) collective-permute-start(bf16[152,896]{1,0:T(8,128)(2,1)S(1)} %get-tuple-element.98), channel_id=1, source_target_pairs={{0,2},{2,4},{4,6},{6,0},{1,3},{3,5},{5,7},{7,1},{8,10},{10,12},{12... | collective-permute-start | bytes 817160 | tf_op jit(solution)/shard_map/ppermute | solution.py:24
  321.2 104.8 %collective-permute-start.93 = (bf16[2,152,896]{2,1,0:T(8,128)(2,1)}, bf16[2,152,896]{2,1,0:T(8,128)(2,1)}, u32[]{:S(2)}, u32[]{:S(2)}) collective-permute-start(bf16[2,152,896]{2,1,0:T(8,128)(2,1)} %get-tuple-element.118), channel_id=1, source_target_pairs={{0,2},{2,4},{4,6},{6,0},{1,3},{3,5},{5,7},{7,1},{8,10},{10,12},{12... | collective-permute-start | bytes 1634312 | tf_op jit(solution)/shard_map/ppermute | solution.py:24
  321.2 105.3 %collective-permute-start.94 = (bf16[2,152,896]{2,1,0:T(8,128)(2,1)}, bf16[2,152,896]{2,1,0:T(8,128)(2,1)}, u32[]{:S(2)}, u32[]{:S(2)}) collective-permute-start(bf16[2,152,896]{2,1,0:T(8,128)(2,1)} %get-tuple-element.120), channel_id=1, source_target_pairs={{0,6},{2,0},{4,2},{6,4},{1,7},{3,1},{5,3},{7,5},{8,14},{10,8},{12,... | collective-permute-start | bytes 1634312 | tf_op jit(solution)/shard_map/ppermute | solution.py:24
  339.6 33.1 %collective-permute-start.84 = (bf16[4,2,28,1216]{3,0,2,1:T(4,128)(2,1)}, bf16[4,2,28,1216]{3,0,2,1:T(4,128)(2,1)S(1)}, u32[]{:S(2)}, u32[]{:S(2)}) collective-permute-start(bf16[4,2,28,1216]{3,0,2,1:T(4,128)(2,1)} %copy.193), channel_id=1, source_target_pairs={{0,2},{2,4},{4,6},{6,0},{1,3},{3,5},{5,7},{7,1},{8,10},{10,12},{12... | collective-permute-start | bytes 1634312 | tf_op jit(solution)/shard_map/ppermute | solution.py:24
  340.8 31.9 %collective-permute-start.85 = (bf16[4,2,28,1216]{3,0,2,1:T(4,128)(2,1)}, bf16[4,2,28,1216]{3,0,2,1:T(4,128)(2,1)S(1)}, u32[]{:S(2)}, u32[]{:S(2)}) collective-permute-start(bf16[4,2,28,1216]{3,0,2,1:T(4,128)(2,1)} %copy.196), channel_id=1, source_target_pairs={{0,6},{2,0},{4,2},{6,4},{1,7},{3,1},{5,3},{7,5},{8,14},{10,8},{12,... | collective-permute-start | bytes 1634312 | tf_op jit(solution)/shard_map/ppermute | solution.py:24
  344.7 30.6 %collective-permute-start.86 = (bf16[4,2,28,1216]{3,0,2,1:T(4,128)(2,1)}, bf16[4,2,28,1216]{3,0,2,1:T(4,128)(2,1)S(1)}, u32[]{:S(2)}, u32[]{:S(2)}) collective-permute-start(bf16[4,2,28,1216]{3,0,2,1:T(4,128)(2,1)} %copy.199), channel_id=1, source_target_pairs={{0,4},{2,6},{4,0},{6,2},{1,5},{3,7},{5,1},{7,3},{8,12},{10,14},{12... | collective-permute-start | bytes 1634312 | tf_op jit(solution)/shard_map/ppermute | solution.py:24
  375.4 23.9 %collective-permute-start.80 = (bf16[4,2,28,1216]{3,0,2,1:T(4,128)(2,1)S(1)}, bf16[4,2,28,1216]{3,0,2,1:T(4,128)(2,1)S(1)}, u32[]{:S(2)}, u32[]{:S(2)}) collective-permute-start(bf16[4,2,28,1216]{3,0,2,1:T(4,128)(2,1)S(1)} %copy.188), channel_id=1, source_target_pairs={{0,16},{8,24},{16,0},{24,8},{1,17},{9,25},{17,1},{25,9},{2,18},{10... | collective-permute-start | bytes 1634312 | tf_op jit(solution)/shard_map/ppermute | solution.py:24
  386.9 18.6 %collective-permute-start.87 = (bf16[2,28,1216]{2,1,0:T(8,128)(2,1)S(1)}, bf16[2,28,1216]{2,1,0:T(8,128)(2,1)S(1)}, u32[]{:S(2)}, u32[]{:S(2)}) collective-permute-start(bf16[2,28,1216]{2,1,0:T(8,128)(2,1)S(1)} %get-tuple-element.140), channel_id=1, source_target_pairs={{0,8},{8,16},{16,24},{24,0},{1,9},{9,17},{17,25},{25,1},{2,10},{10... | collective-permute-start | bytes 408584 | tf_op jit(solution)/shard_map/ppermute | solution.py:24
  386.9 19.2 %collective-permute-start.88 = (bf16[2,28,1216]{2,1,0:T(8,128)(2,1)S(1)}, bf16[2,28,1216]{2,1,0:T(8,128)(2,1)S(1)}, u32[]{:S(2)}, u32[]{:S(2)}) collective-permute-start(bf16[2,28,1216]{2,1,0:T(8,128)(2,1)S(1)} %get-tuple-element.142), channel_id=1, source_target_pairs={{0,24},{8,0},{16,8},{24,16},{1,25},{9,1},{17,9},{25,17},{2,26},{10... | collective-permute-start | bytes 408584 | tf_op jit(solution)/shard_map/ppermute | solution.py:24
  408.4 17.3 %collective-permute-start.83 = (bf16[2,28,1216]{2,1,0:T(8,128)(2,1)S(1)}, bf16[2,28,1216]{2,1,0:T(8,128)(2,1)S(1)}, u32[]{:S(2)}, u32[]{:S(2)}) collective-permute-start(bf16[2,28,1216]{2,1,0:T(8,128)(2,1)S(1)} %get-tuple-element.144), channel_id=1, source_target_pairs={{0,4},{2,6},{4,0},{6,2},{1,5},{3,7},{5,1},{7,3},{8,12},{10,14},{12... | collective-permute-start | bytes 408584 | tf_op jit(solution)/shard_map/ppermute | solution.py:24
  416.6 21.4 %collective-permute-start.55 = (bf16[2,256,896]{2,1,0:T(8,128)(2,1)S(1)}, bf16[2,256,896]{2,1,0:T(8,128)(2,1)S(1)}, u32[]{:S(2)}, u32[]{:S(2)}) collective-permute-start(bf16[2,256,896]{2,1,0:T(8,128)(2,1)S(1)} %pad_maximum_fusion.6), channel_id=1, source_target_pairs={{0,32},{32,0},{1,33},{33,1},{2,34},{34,2},{3,35},{35,3},{4,36},{36... | collective-permute-start | bytes 2752520 | tf_op jit(solution)/shard_map/ppermute | solution.py:24
  448.7 21.9 %collective-permute-start.101 = (bf16[152,896]{1,0:T(8,128)(2,1)S(1)}, bf16[152,896]{1,0:T(8,128)(2,1)}, u32[]{:S(2)}, u32[]{:S(2)}) collective-permute-start(bf16[152,896]{1,0:T(8,128)(2,1)S(1)} %fusion.41), channel_id=1, source_target_pairs={{0,64},{64,0},{1,65},{65,1},{2,66},{66,2},{3,67},{67,3},{4,68},{68... | collective-permute-start | bytes 817160 | tf_op jit(solution)/shard_map/ppermute | solution.py:24
  454.9 16.7 %collective-permute-start.57 = (bf16[256,896]{1,0:T(8,128)(2,1)}, bf16[256,896]{1,0:T(8,128)(2,1)}, u32[]{:S(2)}, u32[]{:S(2)}) collective-permute-start(bf16[256,896]{1,0:T(8,128)(2,1)} %fusion.113), channel_id=1, source_target_pairs={{0,32},{32,0},{1,33},{33,1},{2,34},{34,2},{3,35},{35,3},{4,36},{36... | collective-permute-start | bytes 1376264 | tf_op jit(solution)/shard_map/ppermute | solution.py:24
  471.4 72.5 %collective-permute-start.102 = (bf16[152,896]{1,0:T(8,128)(2,1)}, bf16[152,896]{1,0:T(8,128)(2,1)}, u32[]{:S(2)}, u32[]{:S(2)}) collective-permute-start(bf16[152,896]{1,0:T(8,128)(2,1)} %broadcast_select_fusion.2), channel_id=1, source_target_pairs={{0,32},{32,0},{1,33},{33,1},{2,34},{34,2},{3,35},{35,3},{4,36},{36... | collective-permute-start | bytes 817160 | tf_op jit(solution)/shard_map/ppermute | solution.py:24
  521.0 17.7 %collective-permute-start.59 = (bf16[256,896]{1,0:T(8,128)(2,1)}, bf16[256,896]{1,0:T(8,128)(2,1)S(1)}, u32[]{:S(2)}, u32[]{:S(2)}) collective-permute-start(bf16[256,896]{1,0:T(8,128)(2,1)} %slice.613), channel_id=1, source_target_pairs={{0,32},{32,0},{1,33},{33,1},{2,34},{34,2},{3,35},{35,3},{4,36},{36... | collective-permute-start | bytes 1376264 | tf_op jit(solution)/shard_map/ppermute | solution.py:24
  545.7 34.1 %collective-permute-start.51 = (bf16[256,896]{1,0:T(8,128)(2,1)}, bf16[256,896]{1,0:T(8,128)(2,1)S(1)}, u32[]{:S(2)}, u32[]{:S(2)}) collective-permute-start(bf16[256,896]{1,0:T(8,128)(2,1)} %fusion.30), channel_id=1, source_target_pairs={{0,64},{64,0},{1,65},{65,1},{2,66},{66,2},{3,67},{67,3},{4,68},{68... | collective-permute-start | bytes 1376264 | tf_op jit(solution)/shard_map/ppermute | solution.py:24
  (148 other events, 2198.1 us)
